TPU v7x, 32 devices: a whole 2x2x4 slice. The times are simulated.
32 devices in a mesh: row: 4 (over x, core), col: 8 (over z, y).
Axes of the slice: x: 2, y: 2, z: 4, core: 2. Of those that a mesh axis runs over, the one named last changes fastest.
Arguments:
- centroid: float32 [3, 131072], P(None, ('row', 'col')), may hold values from -6 to 6
- normals: float32 [3, 131072], P(None, ('row', 'col')), may hold values from -3 to 3
- tangent: float32 [3, 131072], P(None, ('row', 'col')), may hold values from -3 to 3
- element_area: float32 [131072], P(('row', 'col')), may hold values from 0.01 to 0.04
- forward_field: float32 [2, 131072], P(None, ('row', 'col')), may hold values from -6 to 6
- adjoint_field: float32 [2, 131072], P(None, ('row', 'col')), may hold values from -6 to 6
- corners: int32 [3, 131072], P(None, ('row', 'col')), may hold values from 0 to 65535, as said below
- slot_map: int32 [65536], replicated, may hold values from 0 to 65535, as said below
- quad_order: int32 [32, 4, 8, 32], P('row', None, 'col'), may hold values from 0 to 2
- morph_modes: float32 [300, 6, 65536], P(None, None, ('row', 'col')), may hold values from -0.3 to 0.3
Outputs:
- vertex_partial: float32 [6, 65536], P(None, ('row', 'col'))
- mode_gradient: float32 [300], replicated
Inputs may be any that keep to these rules, and one draw needn't show every extreme that they name: slot_map is a permutation of 0 to 65535. `corners`: for each shard of elements (elements b * 4096 to (b + 1) * 4096 - 1), its 12288 corner references map through slot_map onto the slots of any one patch at most 384 times, and exactly 384 times for some patch.
All inputs are finite; a program needn't handle non-finite values.
Results may differ from a plain program's by a relative error of at most 0.0003.
Values sent between devices are 32-bit elements; how exact they have to be, the bound alone decides.
No kernel may reach another device: no remote copies, remote signals or barrier semaphores. Data moves between devices by JAX's collectives and lax.ppermute only.
A program may use at most 128 MiB of HBM per device.

v0:
```python
import math

import jax
import jax.numpy as jnp
from jax import lax
from jax.sharding import PartitionSpec as P

SLAB_DEV = 8


wavenumber = 4.0
quad_offsets = (-0.6, 0.0, 0.6)
quad_table = ((0.0, 1.0, 0.0), (0.5, 0.0, 0.5), (1.0 / 3.0, 1.0 / 3.0, 1.0 / 3.0))


def point_weights(pair_flags, point_index):
    weight_sum = jnp.zeros(pair_flags.shape, jnp.float32)
    for flag_level in range(3):
        chosen = jnp.where(pair_flags == flag_level, quad_table[flag_level][point_index], 0.0)
        weight_sum = weight_sum + chosen.astype(jnp.float32)
    return weight_sum


def pair_terms(
    row_point, row_adjoint, col_point, col_normal, col_tangent, col_area, col_forward, pair_flags
):
    row_count = row_point.shape[1]
    col_count = col_point.shape[1]
    row_total = jnp.zeros((3, row_count), jnp.float32)
    col_total = jnp.zeros((3, col_count), jnp.float32)
    normal_total = jnp.zeros((3, col_count), jnp.float32)
    real_coupling = (
        row_adjoint[0][:, None] * col_forward[0][None, :]
        + row_adjoint[1][:, None] * col_forward[1][None, :]
    )
    imag_coupling = (
        row_adjoint[0][:, None] * col_forward[1][None, :]
        - row_adjoint[1][:, None] * col_forward[0][None, :]
    )
    spread = jnp.sqrt(col_area)
    for point_index in range(3):
        weight = point_weights(pair_flags, point_index) * col_area[None, :]
        source = col_point + quad_offsets[point_index] * spread[None, :] * col_tangent
        offset = row_point[:, :, None] - source[:, None, :]
        radius_sq = jnp.sum(offset * offset, axis=0) + col_area[None, :]
        radius = jnp.sqrt(radius_sq)
        phase_arg = wavenumber * radius
        cosine = jnp.cos(phase_arg)
        sine_part = jnp.sin(phase_arg)
        scale_three = 1.0 / (4.0 * math.pi * radius * radius_sq)
        scale_five = scale_three / radius_sq
        first_real = (-cosine - phase_arg * sine_part) * scale_three
        first_imag = (-sine_part + phase_arg * cosine) * scale_three
        poly_real = 3.0 - phase_arg * phase_arg
        poly_imag = -3.0 * phase_arg
        second_real = (cosine * poly_real - sine_part * poly_imag) * scale_five
        second_imag = (sine_part * poly_real + cosine * poly_imag) * scale_five
        along_normal = jnp.sum(offset * col_normal[:, None, :], axis=0)
        combo_real = -first_imag / wavenumber - second_real * along_normal
        combo_imag = first_real / wavenumber - second_imag * along_normal
        coeff_first = (real_coupling * first_real - imag_coupling * first_imag) * weight
        coeff_second = (real_coupling * combo_real - imag_coupling * combo_imag) * weight
        position = coeff_second[None] * offset - coeff_first[None] * col_normal[:, None, :]
        row_total = row_total + jnp.sum(position, axis=2)
        col_total = col_total - jnp.sum(position, axis=1)
        normal_total = normal_total - jnp.sum(coeff_first[None] * offset, axis=1)
    return (row_total, col_total, normal_total)


def body(
    centroid,
    normals,
    tangent,
    element_area,
    forward_field,
    adjoint_field,
    corners,
    slot_map,
    quad_order,
    morph_modes,
):
    local_count = centroid.shape[1]
    col_pack = jnp.concatenate(
        [centroid, normals, tangent, element_area[None, :], forward_field], axis=0
    )
    col_blocks = lax.all_gather(col_pack[None], "row", axis=0, tiled=True)
    slab_pack = jnp.concatenate([centroid[:, :SLAB_DEV], adjoint_field[:, :SLAB_DEV]], axis=0)
    slab_gathered = lax.all_gather(slab_pack, "col", axis=1, tiled=True)
    row_point = slab_gathered[0:3]
    row_adjoint = slab_gathered[3:5]
    block_flags = jnp.transpose(quad_order[:, :, 0, :], (1, 0, 2))
    tile_width = local_count // block_flags.shape[2]

    def visit_block(row_carry, inputs):
        column_block, tile_flags = inputs
        pair_flags = jnp.repeat(jnp.repeat(tile_flags, SLAB_DEV, axis=0), tile_width, axis=1)
        row_total, col_total, normal_total = pair_terms(
            row_point,
            row_adjoint,
            column_block[0:3],
            column_block[3:6],
            column_block[6:9],
            column_block[9],
            column_block[10:12],
            pair_flags,
        )
        return (row_carry + row_total, jnp.concatenate([col_total, normal_total], axis=0))

    row_sum, col_parts = lax.scan(
        visit_block, jnp.zeros(row_point.shape, jnp.float32), (col_blocks, block_flags)
    )
    own_columns = lax.psum_scatter(col_parts, "row", scatter_dimension=0, tiled=True)[0]
    own_rows = lax.psum_scatter(row_sum, "col", scatter_dimension=1, tiled=True)
    row_whole = jnp.pad(own_rows, ((0, 3), (0, local_count - SLAB_DEV)))
    element_part = own_columns + row_whole
    slot_ids = slot_map[corners].reshape(-1)
    values = jnp.concatenate([(element_part / 3.0).T] * 3, axis=0)
    device_total = lax.axis_size(("row", "col"))
    patch_size = slot_map.shape[0] // device_total
    capacity = (3 * local_count + device_total - 1) // device_total
    owner_ids = slot_ids // patch_size
    inside_ids = slot_ids % patch_size
    owner_onehot = (
        owner_ids[:, None] == jnp.arange(device_total, dtype=jnp.int32)[None, :]
    ).astype(jnp.int32)
    bucket_place = jnp.sum((jnp.cumsum(owner_onehot, axis=0) - 1) * owner_onehot, axis=1)
    packed = jnp.concatenate([values, inside_ids.astype(jnp.float32)[:, None]], axis=1)
    outbox = (
        jnp.zeros((device_total, capacity, 7), jnp.float32).at[owner_ids, bucket_place].set(packed)
    )
    inbox = lax.all_to_all(outbox, ("row", "col"), split_axis=0, concat_axis=0, tiled=True)
    received = inbox.reshape(-1, 7)
    received_slot = received[:, 6].astype(jnp.int32)
    vertex_partial = jax.ops.segment_sum(received[:, 0:6], received_slot, num_segments=patch_size).T
    projected = jnp.dot(
        morph_modes.reshape(morph_modes.shape[0], -1),
        vertex_partial.reshape(-1),
        precision=lax.Precision.HIGHEST,
    )
    mode_gradient = lax.psum(projected, ("row", "col"))
    return (vertex_partial, mode_gradient)


def solution(mesh):
    return jax.shard_map(
        body,
        mesh=mesh,
        in_specs=(
            P(None, ("row", "col")),
            P(None, ("row", "col")),
            P(None, ("row", "col")),
            P(("row", "col")),
            P(None, ("row", "col")),
            P(None, ("row", "col")),
            P(None, ("row", "col")),
            P(),
            P("row", None, "col", None),
            P(None, None, ("row", "col")),
        ),
        out_specs=(P(None, ("row", "col")), P()),
        check_vma=False,
    )
```

profile of v0, /device:TPU:0, one launch (start us, length us, event | category | flops | bytes accessed | tf_op | source)
XLA Modules:
  0.0 452.5 jit_solution(16946478535807887005)
XLA Ops:
  8.9 32.2 %all_gather.6 = f32[5,64]{0,1:T(8,128)S(1)} all-gather(f32[5,8]{0,1:T(8,128)S(1)} %pad_maximum_fusion.1), channel_id=1, replica_groups=mesh['row'=4,'col'=8] {'col'}, dimensions={1}, use_global_device_ids=true | all-gather | bytes 1440 | tf_op jit(solution)/shard_map/all_gather | solution.py:88
  41.3 2.8 concatenate.24
  44.1 10.0 %all-gather.1 = f32[4,12,4096]{2,1,0:T(8,128)S(1)} all-gather(f32[1,12,4096]{2,1,0:T(8,128)S(1)} %bitcast.167), channel_id=2, replica_groups=mesh['row'=4,'col'=8] {'row'}, dimensions={0}, use_global_device_ids=true | all-gather | bytes 983040 | tf_op jit(solution)/shard_map/all_gather | solution.py:86
  54.8 101.7 %while.16 = (s32[]{:T(128)}, f32[3,64]{1,0:T(4,128)S(1)}, f32[4,6,4096]{2,1,0:T(8,128)S(1)}, f32[2,64]{1,0:T(2,128)S(1)}, f32[4,12,4096]{2,1,0:T(8,128)S(1)}, /*...) while((s32[]{:T(128)}, f32[3,64]{1,0:T(4,128)S(1)}, ...), condition=%wide.region_19.20_spmd.clone, body=%wide.region_3.19_spmd.clone.sunk | while | flops 65386952 | bytes 32506868 | solution.py:109
  56.1 5.8 %subtract_multiply_fusion.23 = (f32[64,4096]{1,0:T(8,128)S(1)}, f32[64,4096]{1,0:T(8,128)S(1)}) fusion(f32[64,4096]{1,0:T(8,128)S(1)} %get-tuple-element.304, f32[64,4096]{1,0:T(8,128)S(1)} %get-tuple-element.305, f32[8,8,32,128]{3,2,1,0:T(8,128)S(1)} %bitcast.148, f32[4096]{0:T(1024)S(1)} %bitcast.155, f32[4096]{0:T(1024)S(1)} %bitcast.160, ...), kind=kLoop, calls=%fused_computation.52.clone.1 | loop fusion | flops 12582912 | bytes 5292544 | tf_op jit(solution)/shard_map/while/body/eval_jaxpr/mul | solution.py:62
  61.9 3.1 fusion.50
  65.3 11.4 %subtract_multiply_fusion.24 = (f32[64,4096]{1,0:T(8,128)S(1)}, f32[64,4096]{1,0:T(8,128)S(1)}, f32[64,4096]{1,0:T(8,128)S(1)}, f32[64,4096]{1,0:T(8,128)S(1)}) fusion(f32[64,4096]{1,0:T(8,128)S(1)} %get-tuple-element.315, f32[64,4096]{1,0:T(8,128)S(1)} %get-tuple-element.316, f32[8,8,32,128]{3,2,1,0:T(8,128)S(1)} %bitcast.149, ...), kind=kLoop, calls=%fused_computation.36.clone.1 | loop fusion | flops 23592960 | bytes 10535424 | tf_op jit(solution)/shard_map/while/body/eval_jaxpr/mul | solution.py:62
  76.7 3.3 fusion.51
  81.4 5.8 %subtract_multiply_fusion.23 = (f32[64,4096]{1,0:T(8,128)S(1)}, f32[64,4096]{1,0:T(8,128)S(1)}) fusion(f32[64,4096]{1,0:T(8,128)S(1)} %get-tuple-element.304, f32[64,4096]{1,0:T(8,128)S(1)} %get-tuple-element.305, f32[8,8,32,128]{3,2,1,0:T(8,128)S(1)} %bitcast.148, f32[4096]{0:T(1024)S(1)} %bitcast.155, f32[4096]{0:T(1024)S(1)} %bitcast.160, ...), kind=kLoop, calls=%fused_computation.52.clone.1 | loop fusion | flops 12582912 | bytes 5292544 | tf_op jit(solution)/shard_map/while/body/eval_jaxpr/mul | solution.py:62
  87.2 3.1 fusion.50
  90.7 11.4 %subtract_multiply_fusion.24 = (f32[64,4096]{1,0:T(8,128)S(1)}, f32[64,4096]{1,0:T(8,128)S(1)}, f32[64,4096]{1,0:T(8,128)S(1)}, f32[64,4096]{1,0:T(8,128)S(1)}) fusion(f32[64,4096]{1,0:T(8,128)S(1)} %get-tuple-element.315, f32[64,4096]{1,0:T(8,128)S(1)} %get-tuple-element.316, f32[8,8,32,128]{3,2,1,0:T(8,128)S(1)} %bitcast.149, ...), kind=kLoop, calls=%fused_computation.36.clone.1 | loop fusion | flops 23592960 | bytes 10535424 | tf_op jit(solution)/shard_map/while/body/eval_jaxpr/mul | solution.py:62
  102.1 3.3 fusion.51
  106.8 5.8 %subtract_multiply_fusion.23 = (f32[64,4096]{1,0:T(8,128)S(1)}, f32[64,4096]{1,0:T(8,128)S(1)}) fusion(f32[64,4096]{1,0:T(8,128)S(1)} %get-tuple-element.304, f32[64,4096]{1,0:T(8,128)S(1)} %get-tuple-element.305, f32[8,8,32,128]{3,2,1,0:T(8,128)S(1)} %bitcast.148, f32[4096]{0:T(1024)S(1)} %bitcast.155, f32[4096]{0:T(1024)S(1)} %bitcast.160, ...), kind=kLoop, calls=%fused_computation.52.clone.1 | loop fusion | flops 12582912 | bytes 5292544 | tf_op jit(solution)/shard_map/while/body/eval_jaxpr/mul | solution.py:62
  112.6 3.1 fusion.50
  116.1 11.4 %subtract_multiply_fusion.24 = (f32[64,4096]{1,0:T(8,128)S(1)}, f32[64,4096]{1,0:T(8,128)S(1)}, f32[64,4096]{1,0:T(8,128)S(1)}, f32[64,4096]{1,0:T(8,128)S(1)}) fusion(f32[64,4096]{1,0:T(8,128)S(1)} %get-tuple-element.315, f32[64,4096]{1,0:T(8,128)S(1)} %get-tuple-element.316, f32[8,8,32,128]{3,2,1,0:T(8,128)S(1)} %bitcast.149, ...), kind=kLoop, calls=%fused_computation.36.clone.1 | loop fusion | flops 23592960 | bytes 10535424 | tf_op jit(solution)/shard_map/while/body/eval_jaxpr/mul | solution.py:62
  127.5 3.3 fusion.51
  132.2 5.8 %subtract_multiply_fusion.23 = (f32[64,4096]{1,0:T(8,128)S(1)}, f32[64,4096]{1,0:T(8,128)S(1)}) fusion(f32[64,4096]{1,0:T(8,128)S(1)} %get-tuple-element.304, f32[64,4096]{1,0:T(8,128)S(1)} %get-tuple-element.305, f32[8,8,32,128]{3,2,1,0:T(8,128)S(1)} %bitcast.148, f32[4096]{0:T(1024)S(1)} %bitcast.155, f32[4096]{0:T(1024)S(1)} %bitcast.160, ...), kind=kLoop, calls=%fused_computation.52.clone.1 | loop fusion | flops 12582912 | bytes 5292544 | tf_op jit(solution)/shard_map/while/body/eval_jaxpr/mul | solution.py:62
  138.0 3.1 fusion.50
  141.5 11.4 %subtract_multiply_fusion.24 = (f32[64,4096]{1,0:T(8,128)S(1)}, f32[64,4096]{1,0:T(8,128)S(1)}, f32[64,4096]{1,0:T(8,128)S(1)}, f32[64,4096]{1,0:T(8,128)S(1)}) fusion(f32[64,4096]{1,0:T(8,128)S(1)} %get-tuple-element.315, f32[64,4096]{1,0:T(8,128)S(1)} %get-tuple-element.316, f32[8,8,32,128]{3,2,1,0:T(8,128)S(1)} %bitcast.149, ...), kind=kLoop, calls=%fused_computation.36.clone.1 | loop fusion | flops 23592960 | bytes 10535424 | tf_op jit(solution)/shard_map/while/body/eval_jaxpr/mul | solution.py:62
  152.9 3.3 fusion.51
  157.4 68.0 %gather_fusion = s32[12288]{0:T(1024)S(1)} fusion(s32[65536]{0:T(1024)S(1)} %copy-done, s32[12288]{0:T(1024)S(1)} %broadcast_clamp_fusion), kind=kCustom, calls=%fused_computation | custom fusion | bytes 147456 | tf_op jit(solution)/shard_map/gather | solution.py:116
  225.7 9.9 %reduce-window.6 = s32[32,96,128]{2,1,0:T(8,128)S(1)} reduce-window(s32[32,96,128]{2,1,0:T(8,128)S(1)} %fusion.28, s32[]{:T(128)} %constant.154.clone.1), window={size=1x1x128 pad=0_0x0_0x127_0}, to_apply=%region_0.1 | reduce-window | flops 49938432 | bytes 3145732 | tf_op jit(solution)/shard_map/reduce-window
  237.7 21.3 %all-reduce.1 = f32[3,64]{1,0:T(4,128)S(1)} all-reduce(f32[3,64]{1,0:T(4,128)S(1)} %get-tuple-element.114), channel_id=4, replica_groups=mesh['row'=4,'col'=8] {'col'}, use_global_device_ids=true, to_apply=%region_21.22.clone | all-reduce | flops 192 | bytes 1536
  259.0 1.2 fusion.27
  263.4 4.0 copy.37
  267.4 33.8 %scatter_custom_fusion.1 = f32[7,12288]{0,1:T(8,128)} fusion(s32[12288]{0:T(1024)S(1)} %broadcast_select_fusion, f32[12288,7]{1,0:T(8,128)} %copy.37, f32[]{:T(128)} %constant.153.clone.1), kind=kCustom, calls=%fused_computation.87 | custom fusion | bytes 344576
  301.2 4.4 copy.38
  305.6 15.3 %all_to_all.5 = f32[32,384,7]{1,2,0:T(8,128)S(1)} all-to-all(f32[32,384,7]{1,2,0:T(8,128)S(1)} %bitcast.164), channel_id=1, replica_groups=mesh['row'=4,'col'=8] {'row','col'}, dimensions={0} | all-to-all | bytes 688128 | tf_op jit(solution)/shard_map/all_to_all | solution.py:131
  320.9 4.0 copy.39
  324.9 66.2 %scatter_custom_fusion = f32[2048,6]{1,0:T(8,128)S(1)} fusion(s32[12288]{0:T(1024)S(1)} %bitcast.172, f32[12288,6]{1,0:T(8,128)} %copy.39, f32[]{:T(128)} %constant.153.clone.1), kind=kCustom, calls=%fused_computation.98 | custom fusion | flops 73728 | bytes 49664 | tf_op jit(solution)/shard_map/scatter-add | solution.py:134
  392.5 14.7 %convolution_reduce_fusion = f32[300]{0:T(512)S(1)} fusion(f32[6,2048,1]{1,2,0:T(1,128)S(1)} %copy.41, f32[300,6,2048]{2,0,1:T(8,128)} %param.21), kind=kOutput, calls=%fused_computation.97 | convolution fusion | flops 44236800 | bytes 14795952 | tf_op jit(solution)/shard_map/dot_general | solution.py:135
  407.1 38.5 %psum.7 = f32[300]{0:T(512)} all-reduce(f32[300]{0:T(512)S(1)} %convolution_reduce_fusion), channel_id=1, replica_groups=mesh['row'=4,'col'=8] {'row','col'}, use_global_device_ids=true, to_apply=%region_24.25 | all-reduce | flops 300 | bytes 2400 | tf_op jit(solution)/shard_map/psum | solution.py:140
  (107 shorter events, 15.9 us)
Async XLA Ops:
  7.2 150.2 %copy-start = (s32[65536]{0:T(1024)S(1)}, s32[65536]{0:T(1024)}, u32[]{:S(2)}) copy-start(s32[65536]{0:T(1024)} %param.19) | copy-start | bytes 786436
  7.2 255.2 %reduce-scatter.3.cloned.1.call-start = ((), (), s32[]{:S(2)}) async-start(), calls=%async_computation.2 | async-start | bytes 655360 | tf_op jit(solution)/shard_map/reduce_scatter | solution.py:112
  54.8 102.5 %copy-start.2 = (s32[3,4096]{1,0:T(4,128)S(1)}, s32[3,4096]{1,0:T(4,128)}, u32[]{:S(2)}) copy-start(s32[3,4096]{1,0:T(4,128)} %param.18) | copy-start | bytes 147460
  156.5 0.8 copy-start.1
  235.6 24.9 %copy-start.5 = (u32[32]{0:T(128)S(1)}, u32[32]{0:T(128)}, u32[]{:S(2)}) copy-start(u32[32]{0:T(128)} %constant.177) | copy-start | bytes 388
  235.6 26.2 %copy-start.4 = (s32[2]{0:T(128)S(1)}, s32[2]{0:T(128)}, u32[]{:S(2)}) copy-start(s32[2]{0:T(128)} %constant.167) | copy-start | bytes 28
  235.6 26.4 %copy-start.3 = (s32[2]{0:T(128)S(1)}, s32[2]{0:T(128)}, u32[]{:S(2)}) copy-start(s32[2]{0:T(128)} %constant.170) | copy-start | bytes 28
Sparse Core Ops, SparseCore 0:
  157.4 21.6 reduce-scatter.2
where the time goes:
time: 453 us
  other arithmetic  178 us (39%)
  local copies, waits for them, and re-layouts  126 us (28%)
  blocking collectives  117 us (26%)
  between operations  14.9 us (3%)
  matrix products  14.7 us (3%)
    mul x8, other arithmetic, pair_terms(): (real_coupling * combo_real - imag_coupling * combo_imag) * weight  68.7 us
    gather x1, local copies, waits for them, and re-layouts, body(): slot_ids = slot_map[corners].reshape(-1)  68 us
    scatter-add x1, other arithmetic, body(): jax.ops.segment_sum(received[:, 0:6], received_slot, num_segments=patch_s...  66.2 us
    unnamed x22, local copies, waits for them, and re-layouts  41.7 us
    psum x1, blocking collectives, body(): mode_gradient = lax.psum(projected, ('row', 'col'))  38.5 us
    all_gather x1, blocking collectives, body(): slab_gathered = lax.all_gather(slab_pack, 'col', axis=1, tiled=True)  32.2 us
    reduce_sum x8, other arithmetic, pair_terms(): col_total = col_total - jnp.sum(position, axis=1)  25.7 us
    unnamed x1, blocking collectives  21.3 us
  transfers between devices with their start and end apart: 1, of which 0 were waited for; matrix products, arithmetic and copies ran while one was open for 18% of the time, Pallas kernels for 0%

commit v1 on v0

v1 whole, which is shorter than its diff:
```python
import functools
import math

import jax
import jax.numpy as jnp
import numpy as np
from jax import lax
from jax.experimental import pallas as pl
from jax.experimental.pallas import tpu as pltpu
from jax.sharding import PartitionSpec as P

SLAB_DEV = 8
LANES = 128
WAVE = 4.0
OFFSET = 0.6
FLAG_WEIGHTS = (1.0, 0.5, 1.0 / 3.0)
GROUPS = (16, 8, 6)
F32 = jnp.float32
BF16 = jnp.bfloat16
AXES = ("row", "col")


def fit_even(fn, degree):
    series = np.polynomial.chebyshev.Chebyshev.interpolate(
        lambda u: fn(np.sqrt(np.maximum(u, 1e-30))), degree, domain=[0, 0.25]
    )
    return [float(x) for x in series.convert(kind=np.polynomial.Polynomial).coef]


SIN_HALF = fit_even(lambda f: math.sqrt(2) * np.sin(np.pi * f) / f, 3)
COS_HALF = fit_even(lambda f: math.sqrt(2) * np.cos(np.pi * f), 3)


def horner(coefs, u):
    total = coefs[-1] * u + coefs[-2]
    for c in coefs[-3::-1]:
        total = total * u + c
    return total


def iota(shape, dim):
    return lax.broadcasted_iota(jnp.int32, shape, dim)


def dot_lanes(a, b, **kw):
    return lax.dot_general(a, b, (((1,), (1,)), ((), ())), preferred_element_type=F32, **kw)


def split(x):
    high = x.astype(BF16)
    return high, (x - high.astype(F32)).astype(BF16)


def plan_kernel(devices, cap, corner_ref, table_ref, hp_ref, lp_ref, out_ref, slot, scat, order):
    count = corner_ref.shape[1]
    rows = table_ref.shape[0]
    patch = rows * LANES // devices
    tiles = -(-cap // LANES)
    table = table_ref[...]
    low = (table & 255).astype(F32)
    both = jnp.concatenate([(table.astype(F32) - low).T, low.T], axis=0).astype(BF16)
    width = min(1024, count)
    half = min(rows, 256)
    hi_iota = iota((half, width), 0).astype(F32).astype(BF16)
    lo_iota = iota((LANES, width), 0)
    for n in range(3):

        def look(i, carry, n=n):
            at = pl.ds(pl.multiple_of(i * width, LANES), width)
            c = corner_ref[n : n + 1, at]
            hi = (c >> 7).astype(F32)
            lo = c & 127
            hot = jnp.concatenate(
                [
                    jnp.where(hi_iota == (hi - float(g)).astype(BF16), 1.0, 0.0).astype(BF16)
                    for g in range(0, rows, half)
                ],
                axis=0,
            )
            found = jnp.dot(both, hot, preferred_element_type=F32)
            found = found[:LANES] + found[LANES:]
            slot[n : n + 1, at] = jnp.sum(
                jnp.where(lo_iota == lo, found, 0.0), axis=0, keepdims=True
            )
            return carry

        lax.fori_loop(0, count // width, look, 0)
    chunk = 256
    tri = jnp.where(iota((chunk, chunk), 0) <= iota((chunk, chunk), 1), 1.0, 0.0).astype(BF16)
    own_iota = iota((devices, chunk), 0).astype(F32)
    carry = jnp.zeros((devices, 1), F32)
    for n in range(3):
        for i in range(count // chunk):
            at = slice(i * chunk, (i + 1) * chunk)
            s = slot[n : n + 1, at]
            owner = jnp.floor((s + 0.5) * (1.0 / patch))
            mask = own_iota == owner
            pre = jnp.dot(
                jnp.where(mask, 1.0, 0.0).astype(BF16), tri, preferred_element_type=F32
            )
            rank = jnp.sum(jnp.where(mask, pre + carry, 0.0), axis=0, keepdims=True) - 1.0
            carry = carry + pre[:, chunk - 1 :]
            tile = jnp.floor((rank + 0.5) * (1.0 / LANES))
            pair = jnp.floor((owner + 0.5) * 0.5)
            hp_ref[n : n + 1, at] = pair * tiles + tile
            lp_ref[n : n + 1, at] = (owner - 2.0 * pair) * LANES + rank - tile * LANES
    units = devices // 2 * tiles
    unit_iota = iota((units, width), 0).astype(F32)
    lane_iota = iota((256, width), 0).astype(F32).astype(BF16)
    scat[...] = jnp.zeros(scat.shape, F32)
    for n in range(3):

        def put(i, carry, n=n):
            at = pl.ds(pl.multiple_of(i * width, LANES), width)
            s = slot[n : n + 1, at]
            inside = s - jnp.floor((s + 0.5) * (1.0 / patch)) * patch
            big = jnp.floor((inside + 0.5) * (1.0 / 256.0)) * 256.0
            mask = unit_iota == hp_ref[n : n + 1, at]
            lhs = jnp.concatenate(
                [jnp.where(mask, big, 0.0), jnp.where(mask, inside - big, 0.0)], axis=0
            ).astype(BF16)
            hot = jnp.where(lane_iota == lp_ref[n : n + 1, at].astype(BF16), 1.0, 0.0).astype(BF16)
            got = dot_lanes(lhs, hot)
            got = got[:units] + got[units:]
            scat[0] += got[:, :LANES]
            scat[1] += got[:, LANES:]
            return carry

        lax.fori_loop(0, count // width, put, 0)
    for b in range(2):
        for j in range(tiles):
            order[j, pl.ds(b, devices // 2, stride=2), :] = scat[
                b, pl.ds(j, devices // 2, stride=tiles), :
            ]
    for j in range(tiles):
        out_ref[:, j * LANES : (j + 1) * LANES] = order[j]
    lane = iota((1, LANES), 1)
    slab = slot[0:1, 0:LANES]
    for n in (1, 2):
        slab = jnp.where(
            lane < n * SLAB_DEV, slab, pltpu.roll(slot[n : n + 1, 0:LANES], n * SLAB_DEV, 1)
        )
    out_ref[:, tiles * LANES :] = jnp.broadcast_to(slab, (devices, LANES))


def plan(corners, table, devices, cap):
    count = corners.shape[1]
    tiles = -(-cap // LANES)
    return pl.pallas_call(
        functools.partial(plan_kernel, devices, cap),
        out_shape=(
            jax.ShapeDtypeStruct((3, count), F32),
            jax.ShapeDtypeStruct((3, count), F32),
            jax.ShapeDtypeStruct((devices, (tiles + 1) * LANES), F32),
        ),
        scratch_shapes=[
            pltpu.VMEM((3, count), F32),
            pltpu.VMEM((2, devices // 2 * tiles, LANES), F32),
            pltpu.VMEM((tiles, devices, LANES), F32),
        ],
        compiler_params=pltpu.CompilerParams(vmem_limit_bytes=24 << 20),
        name="plan",
    )(corners, table)


def point(dist_sq, normal_dot, cr, ci):
    inv = lax.rsqrt(dist_sq)
    turns = (dist_sq * inv) * (0.5 / math.pi)
    inv_sq3 = (inv * 3.0) * inv
    frac = turns - jnp.round(turns)
    u = frac * frac
    s = frac * horner(SIN_HALF, u)
    c = horner(COS_HALF, u)
    er = inv_sq3 - (s * s) * inv_sq3
    ei = (s * c) * inv_sq3
    wr = cr * er - ci * ei
    wi = cr * ei + ci * er
    near = wr * inv
    a = near + wi
    b = (wi * inv - wr) + normal_dot * (near - a * inv_sq3)
    return a, b


def work_list(flags, ids_ref, devices):
    ones = jnp.concatenate([jnp.where(flags == f, 1.0, 0.0) for f in range(3)], axis=0)
    ii = iota((LANES, LANES), 0)
    tri = jnp.where(ii < iota((LANES, LANES), 1), 1.0, 0.0).astype(BF16)
    before = jnp.dot(ones.astype(BF16), tri, preferred_element_type=F32)
    total = jnp.dot(ones.astype(BF16), jnp.ones((LANES, LANES), BF16), preferred_element_type=F32)
    run = jnp.zeros((1, LANES), F32)
    place = jnp.zeros((8, LANES), F32)
    row = iota((8, LANES), 0)
    bounds = []
    for f, size in enumerate(GROUPS):
        start = run
        offset = jnp.zeros((8, LANES), F32)
        for r in range(8):
            offset = jnp.where(row == r, run, offset)
            run = run + total[f * 8 + r : f * 8 + r + 1]
        steps = jnp.floor((run - start + (size - 0.5)) * (1.0 / size))
        bounds += [start, steps]
        run = start + steps * size
        place = place + ones[f * 8 : f * 8 + 8] * (before[f * 8 : f * 8 + 8] + offset)
    place = place.astype(jnp.int32)
    hi, lo = place >> 7, place & 127
    hi_iota = iota((16, LANES), 0)
    got = jnp.zeros((32, LANES), F32)
    for r in range(8):
        hot = jnp.where(ii == lo[r : r + 1], 1.0, 0.0).astype(BF16)
        mask = hi_iota == hi[r : r + 1]
        lhs = jnp.concatenate(
            [jnp.where(mask, ids_ref[k, r : r + 1, :], 0.0) for k in range(2)], axis=0
        )
        got = got + dot_lanes(lhs.astype(BF16), hot)
    shard = got[:16].astype(jnp.int32)
    bounds = [b.astype(jnp.int32) for b in bounds] + [jnp.zeros((2, LANES), jnp.int32)]
    return (
        jnp.where(shard == 0, devices, shard - 1),
        got[16:].astype(jnp.int32),
        jnp.concatenate(bounds, axis=0),
    )


def pair_kernel(
    mesh_shape,
    tiles,
    col_ref,
    inbox_ref,
    ids_ref,
    centroid_ref,
    normals_ref,
    tangent_ref,
    area_ref,
    forward_ref,
    val_ref,
    row_ref,
    tgt,
    src,
    col,
    row,
    list_vmem,
    todo,
    sem,
):
    n_row, n_col = mesh_shape
    devices = n_row * n_col
    mine = col_ref[0]
    flag_rows = 8 // n_row
    flags = []
    for r in range(n_row):
        block = inbox_ref[r * n_col : (r + 1) * n_col, LANES : (1 + flag_rows) * LANES]
        block = jnp.where(iota(block.shape, 0) == mine, block, 0.0)
        block = jnp.sum(block, axis=0, keepdims=True)
        flags += [block[:, h * LANES : (h + 1) * LANES] for h in range(flag_rows)]
    flags = jnp.concatenate(flags, axis=0)
    shard, tile, bounds = work_list(flags, ids_ref, devices)
    list_vmem[0:16, :] = shard
    list_vmem[16:32, :] = tile
    list_vmem[32:40, :] = bounds
    copy = pltpu.make_async_copy(list_vmem, todo, sem)
    copy.start()
    words = inbox_ref[:, 0:LANES].T
    for d in range(devices):
        for k in range(5):
            w = words[k * 8 : k * 8 + 8, d : d + 1] * (WAVE if k < 3 else 1.0)
            tgt[d, k] = jnp.broadcast_to(w, (8, LANES))
    zero = jnp.zeros((8, LANES), F32)
    for k in range(5):
        tgt[devices, k] = zero

    def prepare(t, carry):
        at = pl.ds(pl.multiple_of(t * LANES, LANES), LANES)

        def load(ref, k):
            return jnp.broadcast_to(ref[k : k + 1, at], (8, LANES))

        area = jnp.broadcast_to(area_ref[pl.ds(t, 1), :], (8, LANES))
        spread = jnp.sqrt(area) * (WAVE * OFFSET)
        u = [load(tangent_ref, k) * spread for k in range(3)]
        n = [load(normals_ref, k) * (WAVE * WAVE) for k in range(3)]
        for k in range(3):
            src[t, k] = load(centroid_ref, k) * WAVE
            src[t, 3 + k] = n[k]
            src[t, 6 + k] = u[k]
        src[t, 9] = area * (WAVE * WAVE)
        src[t, 10] = u[0] * u[0] + u[1] * u[1] + u[2] * u[2]
        src[t, 11] = u[0] * n[0] + u[1] * n[1] + u[2] * n[2]
        scale = area * (WAVE**3 / (4.0 * math.pi) / 3.0)
        src[t, 12] = load(forward_ref, 0) * scale
        src[t, 13] = load(forward_ref, 1) * scale
        for k in range(9):
            col[t, k] = zero
        return carry

    lax.fori_loop(0, tiles, prepare, 0)

    def clear(d, carry):
        for k in range(3):
            row[d, k] = zero
        return carry

    lax.fori_loop(0, devices + 1, clear, 0)
    copy.wait()
    for f, size in enumerate(GROUPS):
        start = todo[32 + 2 * f, 0]

        def step(i, carry, f=f, size=size, start=start):
            for g in range(size):
                p = start + i * size + g
                d = todo[p >> 7, p & 127]
                t = todo[16 + (p >> 7), p & 127]
                diff = [tgt[d, k] - src[t, k] for k in range(3)]
                dist = diff[0] * diff[0] + diff[1] * diff[1] + diff[2] * diff[2] + src[t, 9]
                n = [src[t, 3 + k] for k in range(3)]
                along = diff[0] * n[0] + diff[1] * n[1] + diff[2] * n[2]
                ar, ai = tgt[d, 3], tgt[d, 4]
                if f:
                    ar = ar * FLAG_WEIGHTS[f]
                    ai = ai * FLAG_WEIGHTS[f]
                fr, fi = src[t, 12], src[t, 13]
                cr = ar * fr + ai * fi
                ci = ar * fi - ai * fr
                if f == 0:
                    sa, sb = point(dist, along, cr, ci)
                else:
                    u = [src[t, 6 + k] for k in range(3)]
                    cross = diff[0] * u[0] + diff[1] * u[1] + diff[2] * u[2]
                    cross = cross + cross
                    base = dist + src[t, 10]
                    a0, b0 = point(base + cross, along + src[t, 11], cr, ci)
                    a2, b2 = point(base - cross, along - src[t, 11], cr, ci)
                    sa, sb, da, db = a0 + a2, b0 + b2, a0 - a2, b0 - b2
                    if f == 2:
                        a1, b1 = point(dist, along, cr, ci)
                        sa, sb = sa + a1, sb + b1
                moved = [sb * diff[k] for k in range(3)]
                for k in range(3):
                    col[t, k] += moved[k]
                    col[t, 3 + k] += sa * diff[k]
                col[t, 6] += sa
                if f:
                    col[t, 7] += db
                    col[t, 8] += da
                for k in range(3):
                    part = moved[k] + sa * n[k]
                    if f:
                        part = part + db * u[k]
                    row[d, k] += part
            return carry

        lax.fori_loop(0, todo[33 + 2 * f, 0], step, 0)
    scale_p = 1.0 / (3.0 * WAVE * WAVE)
    scale_n = 1.0 / (3.0 * WAVE)

    def finish(t, carry):
        at = pl.ds(pl.multiple_of(t * LANES, LANES), LANES)
        s = [jnp.sum(col[t, k], axis=0, keepdims=True) for k in range(9)]
        for k in range(3):
            u = src[t, 6 + k, 0:1]
            n = src[t, 3 + k, 0:1]
            val_ref[k : k + 1, at] = (s[k] + u * s[7] + n * s[6]) * -scale_p
            val_ref[3 + k : 4 + k, at] = (s[3 + k] + u * s[8]) * scale_n
        return carry

    lax.fori_loop(0, tiles, finish, 0)
    ones = jnp.full((8, LANES), scale_p, F32)
    for k in range(3):
        sums = dot_lanes(
            ones, row[0:devices, k].reshape(devices * 8, LANES), precision=lax.Precision.HIGHEST
        )
        row_ref[k : k + 1, :] = sums[0:1]


def pairs(mesh_shape, mine, inbox, centroid, normals, tangent, area, forward):
    n_row, n_col = mesh_shape
    devices = n_row * n_col
    count = centroid.shape[1]
    tiles = count // LANES
    word = np.arange(devices * tiles)
    per_row = devices // n_row
    ids = np.stack([word // tiles + 1, word % tiles]).astype(np.float32).reshape(2, 8, LANES)
    assert per_row * tiles * n_row == 8 * LANES
    vmem = pl.BlockSpec(memory_space=pltpu.VMEM)
    return pl.pallas_call(
        functools.partial(pair_kernel, mesh_shape, tiles),
        in_specs=[pl.BlockSpec(memory_space=pltpu.SMEM)] + [vmem] * 7,
        out_shape=(
            jax.ShapeDtypeStruct((6, count), F32),
            jax.ShapeDtypeStruct((3, SLAB_DEV * devices), F32),
        ),
        scratch_shapes=[
            pltpu.VMEM((devices + 1, 5, 8, LANES), F32),
            pltpu.VMEM((tiles, 14, 8, LANES), F32),
            pltpu.VMEM((tiles, 9, 8, LANES), F32),
            pltpu.VMEM((devices + 1, 3, 8, LANES), F32),
            pltpu.VMEM((40, LANES), jnp.int32),
            pltpu.SMEM((40, LANES), jnp.int32),
            pltpu.SemaphoreType.DMA(()),
        ],
        compiler_params=pltpu.CompilerParams(vmem_limit_bytes=24 << 20),
        name="pairs",
    )(mine, inbox, jnp.asarray(ids), centroid, normals, tangent, area, forward)


def bucket_kernel(devices, cap, rows, val_ref, part_ref, hp_ref, lp_ref, out_ref, acc):
    count = val_ref.shape[1]
    tiles = -(-cap // LANES)
    units = devices // 2 * tiles
    width = min(1024, count)
    acc[...] = jnp.zeros(acc.shape, F32)
    lane_iota = iota((256, width), 0).astype(F32).astype(BF16)
    unit = (iota((16, width), 0) >> 3).astype(F32).astype(BF16)
    for n in range(3):

        def put(i, carry, n=n):
            at = pl.ds(pl.multiple_of(i * width, LANES), width)
            v = val_ref[:, at]
            v = jnp.concatenate([v, jnp.zeros((2, width), F32)], axis=0)
            v = jnp.concatenate([v, v], axis=0)
            high, low = split(v)
            hp = hp_ref[n : n + 1, at]
            masks = [unit == (hp - 2.0 * q).astype(BF16) for q in range(units // 2)]
            zero = jnp.zeros((16, width), BF16)
            lhs = jnp.concatenate(
                [jnp.where(m, part, zero) for part in (high, low) for m in masks], axis=0
            )
            hot = jnp.where(lane_iota == lp_ref[n : n + 1, at].astype(BF16), 1.0, 0.0).astype(BF16)
            acc[...] += dot_lanes(lhs, hot)
            return carry

        lax.fori_loop(0, count // width, put, 0)
    packed = 2 * tiles * LANES == part_ref.shape[0] * part_ref.shape[1]
    row = iota((8, LANES), 0)
    for j in range(tiles):
        if packed:
            part = jnp.where(
                row == 6,
                part_ref[j : j + 1, 0:LANES],
                part_ref[j : j + 1, LANES : 2 * LANES],
            )
        for o in range(devices):
            q = ((o // 2) * tiles + j) * 8
            lanes = slice((o % 2) * LANES, (o % 2 + 1) * LANES)
            got = acc[q : q + 8, lanes] + acc[units * 8 + q : units * 8 + q + 8, lanes]
            if packed:
                got = jnp.where(row < 6, got, part)
            out_ref[o, j * 8 : j * 8 + 8, :] = got
    if not packed:
        for r in range(rows - 8 * tiles):
            per = part_ref.shape[1] // LANES
            c, h = r // per, r % per
            line = part_ref[c : c + 1, h * LANES : (h + 1) * LANES]
            for o in range(devices):
                out_ref[o, 8 * tiles + r : 8 * tiles + r + 1, :] = line


def message_rows(devices, cap):
    tiles = -(-cap // LANES)
    extra = 3 * SLAB_DEV * devices // LANES
    return 8 * tiles + (0 if extra == 2 * tiles else extra)


def bucket(val, part, hp, lp, devices, cap):
    tiles = -(-cap // LANES)
    rows = message_rows(devices, cap)
    return pl.pallas_call(
        functools.partial(bucket_kernel, devices, cap, rows),
        out_shape=jax.ShapeDtypeStruct((devices, rows, LANES), F32),
        scratch_shapes=[pltpu.VMEM((devices // 2 * tiles * 16, 256), F32)],
        compiler_params=pltpu.CompilerParams(vmem_limit_bytes=32 << 20),
        name="bucket",
    )(val, part, hp, lp)


def owner_kernel(
    devices, cap, me_ref, inbox_ref, slots_ref, morph_ref, vertex_ref, out_ref, lhs, rhs, lines
):
    patch = vertex_ref.shape[1]
    modes = morph_ref.shape[0]
    tiles = -(-cap // LANES)
    his = patch // 256
    me = me_ref[0]
    lane_iota = iota((256, LANES), 0).astype(F32).astype(BF16)
    unit = (iota((16, LANES), 0) >> 3).astype(F32)
    zero = jnp.zeros((16, LANES), BF16)

    def place(k, v, inside):
        hi = jnp.floor((inside + 0.5) * (1.0 / 256.0))
        hot = jnp.where(lane_iota == (inside - hi * 256.0).astype(BF16), 1.0, 0.0)
        at = pl.ds(pl.multiple_of(k * LANES, LANES), LANES)
        rhs[:, at] = hot.astype(BF16)
        high, low = split(jnp.concatenate([v, v], axis=0))
        for q in range(his // 2):
            mask = unit == hi - 2.0 * q
            lhs[q * 16 : q * 16 + 16, at] = jnp.where(mask, high, zero)
            lhs[his * 8 + q * 16 : his * 8 + q * 16 + 16, at] = jnp.where(mask, low, zero)

    packed = inbox_ref.shape[1] == 8 * tiles
    wide = SLAB_DEV * devices // LANES

    def source(block, sums):
        around = pl.ds(pl.multiple_of(block * 8, 8), 8)
        inside = [slots_ref[around, j * LANES : (j + 1) * LANES] for j in range(tiles)]
        if cap % LANES:
            lane = iota((8, LANES), 1)
            inside = [jnp.where(lane < cap - j * LANES, x, -1.0) for j, x in enumerate(inside)]
        for r in range(8):
            s = block * 8 + r
            for j in range(tiles):
                place(s * tiles + j, inbox_ref[s, j * 8 : j * 8 + 8, :], inside[j][r : r + 1])
            if packed:
                sums = tuple(x + inbox_ref[s, j * 8 : j * 8 + 8, :] for j, x in enumerate(sums))
            else:
                sums = (sums[0] + inbox_ref[s, 8 * tiles :, :],)
        return sums

    if packed:
        sums = tuple(jnp.zeros((8, LANES), F32) for _ in range(tiles))
    else:
        sums = (jnp.zeros((3 * wide, LANES), F32),)
    sums = lax.fori_loop(0, devices // 8, source, sums)
    own = slots_ref[:, tiles * LANES : (tiles + 1) * LANES]
    big = jnp.floor((own + 0.5) * (1.0 / 256.0))
    own = jnp.concatenate([big, own - 256.0 * big], axis=0).astype(BF16)
    word = iota((LANES, SLAB_DEV * devices), 0)
    lane = iota((LANES, SLAB_DEV * devices), 1)
    here = iota((devices, SLAB_DEV * devices), 0) == (
        iota((devices, SLAB_DEV * devices), 1) // SLAB_DEV
    )
    base = (me * patch).astype(F32)
    for n in range(3):
        pick = jnp.where(word == n * SLAB_DEV + lane % SLAB_DEV, 1.0, 0.0).astype(BF16)
        got = jnp.dot(own, pick, preferred_element_type=F32)
        got = got[:devices] * 256.0 + got[devices:]
        slot = jnp.sum(jnp.where(here, got, 0.0), axis=0, keepdims=True) - base
        for h in range(wide):
            lines_v = []
            for c in range(3):
                if packed:
                    lines_v.append(sums[c][6 + h : 7 + h])
                else:
                    lines_v.append(sums[0][c * wide + h : c * wide + h + 1])
            v = jnp.concatenate(lines_v + [jnp.zeros((5, LANES), F32)], axis=0)
            place(devices * tiles + n * wide + h, v, slot[:, h * LANES : (h + 1) * LANES])
    both = dot_lanes(lhs[...], rhs[...])
    both = both[: his * 8] + both[his * 8 :]
    for q in range(his):
        vertex_ref[:, q * 256 : (q + 1) * 256] = both[q * 8 : q * 8 + 6]

    lines[...] = jnp.zeros(lines.shape, F32)
    vert = [vertex_ref[:, q * LANES : (q + 1) * LANES] for q in range(patch // LANES)]

    def project(m, carry):
        terms = [morph_ref[m, :, q * LANES : (q + 1) * LANES] * v for q, v in enumerate(vert)]
        while len(terms) > 1:
            terms = [a + b for a, b in zip(terms[::2], terms[1::2])]
        lines[pl.ds(m, 1), :] = jnp.sum(terms[0], axis=0, keepdims=True)
        return carry

    lax.fori_loop(0, modes, project, 0, unroll=4)
    ones = jnp.ones((8, LANES), F32)
    sums = dot_lanes(ones, lines[...], precision=lax.Precision.HIGHEST)
    for o in range(0, devices, 8):
        out_ref[o : o + 8, :] = sums


def owner(me, inbox, slots, morph, devices, cap):
    modes, _, patch = morph.shape
    tiles = -(-cap // LANES)
    depth = (devices * tiles + 3 * SLAB_DEV * devices // LANES) * LANES
    words = -(-modes // LANES) * LANES
    vmem = pl.BlockSpec(memory_space=pltpu.VMEM)
    return pl.pallas_call(
        functools.partial(owner_kernel, devices, cap),
        in_specs=[pl.BlockSpec(memory_space=pltpu.SMEM), vmem, vmem, vmem],
        out_shape=(
            jax.ShapeDtypeStruct((6, patch), F32),
            jax.ShapeDtypeStruct((devices, words), F32),
        ),
        scratch_shapes=[
            pltpu.VMEM((patch // 256 * 16, depth), BF16),
            pltpu.VMEM((256, depth), BF16),
            pltpu.VMEM((words, LANES), F32),
        ],
        compiler_params=pltpu.CompilerParams(vmem_limit_bytes=48 << 20),
        name="owner",
    )(me, inbox, slots, morph)


def swap(x):
    return lax.all_to_all(x, AXES, split_axis=0, concat_axis=0, tiled=True)


def body(
    centroid,
    normals,
    tangent,
    element_area,
    forward_field,
    adjoint_field,
    corners,
    slot_map,
    quad_order,
    morph_modes,
):
    n_row, n_col = lax.axis_size("row"), lax.axis_size("col")
    devices = n_row * n_col
    count = centroid.shape[1]
    cap = -(-3 * count // devices)
    mine = lax.axis_index("col").astype(jnp.int32).reshape(1)
    me = lax.axis_index(AXES).astype(jnp.int32).reshape(1)

    slab = jnp.concatenate([centroid[:, :SLAB_DEV], adjoint_field[:, :SLAB_DEV]], axis=0)
    slab = jnp.pad(slab.reshape(-1), (0, LANES - 5 * SLAB_DEV))
    flags = jnp.transpose(quad_order[:, :, 0, :], (1, 0, 2)).reshape(n_row, 1, -1).astype(F32)
    flags = jnp.broadcast_to(flags, (n_row, n_col, flags.shape[2])).reshape(devices, -1)
    first = jnp.concatenate([jnp.broadcast_to(slab[None], (devices, LANES)), flags], axis=1)
    first = swap(first)

    hp, lp, slots = plan(corners, slot_map.reshape(-1, LANES), devices, cap)
    slots = swap(slots)

    val, part = pairs(
        (n_row, n_col),
        mine,
        first,
        centroid,
        normals,
        tangent,
        element_area.reshape(-1, LANES),
        forward_field,
    )
    inbox = swap(bucket(val, part, hp, lp, devices, cap))
    vertex_partial, sums = owner(me, inbox, slots, morph_modes, devices, cap)
    mode_gradient = jnp.sum(swap(sums), axis=0)[: morph_modes.shape[0]]
    return (vertex_partial, mode_gradient)


def solution(mesh):
    return jax.shard_map(
        body,
        mesh=mesh,
        in_specs=(
            P(None, ("row", "col")),
            P(None, ("row", "col")),
            P(None, ("row", "col")),
            P(("row", "col")),
            P(None, ("row", "col")),
            P(None, ("row", "col")),
            P(None, ("row", "col")),
            P(),
            P("row", None, "col", None),
            P(None, None, ("row", "col")),
        ),
        out_specs=(P(None, ("row", "col")), P()),
        check_vma=False,
    )
```

time: 453 us -> 126 us (0.28)
  other arithmetic: 178 us -> 1.39 us
  blocking collectives: 117 us -> 12.7 us
  local copies, waits for them, and re-layouts: 126 us -> 27.2 us
  Pallas kernels: 0 us -> 63.7 us
  starting transfers between devices: 0.04 us -> 19.3 us
  matrix products: 14.7 us -> 0 us
  between operations: 14.9 us -> 0.73 us
    mul x12 -> x0, other arithmetic: 68.8 us -> none  [the longest x8 68.7 us: pair_terms(): (real_coupling * combo_real - imag_coupling * combo_imag) * weight]
    gather x1 -> x0, local copies, waits for them, and re-layouts: 68 us -> none  [body(): slot_ids = slot_map[corners].reshape(-1)]
    scatter-add x1 -> x0, other arithmetic: 66.2 us -> none  [body(): jax.ops.segment_sum(received[:, 0:6], received_slot, num_segments=patch_s...]
    pallas_call x0 -> x4, Pallas kernels: none -> 63.7 us  [the longest x1 25.3 us: pairs(): pl.pallas_call(functools.partial(pair_kernel, mesh_shape, tiles), in_spec...]
    all_gather x2 -> x0, blocking collectives: 42.2 us -> none  [the longest x1 32.2 us: body(): slab_gathered = lax.all_gather(slab_pack, 'col', axis=1, tiled=True)]
    psum x1 -> x0, blocking collectives: 38.5 us -> none  [body(): mode_gradient = lax.psum(projected, ('row', 'col'))]
    reduce_sum x13 -> x1, other arithmetic: 29.6 us -> 0.64 us  [body(): mode_gradient = jnp.sum(swap(sums), axis=0)[:morph_modes.shape[0]]]
    unnamed x1 -> x0, blocking collectives: 21.3 us -> none
  transfers between devices with their start and end apart: 1 -> 3, of which waited for: 0 -> 0; matrix products, arithmetic and copies ran while one was open for 18% -> 15% of each run, Pallas kernels for 0% -> 37%
where the time goes in v1:
time: 126 us; the launch traced here: 125 us
  Pallas kernels  63.7 us (51%)
  local copies, waits for them, and re-layouts  27.2 us (22%)
  starting transfers between devices  19.3 us (15%)
  blocking collectives  12.7 us (10%)
  other arithmetic  1.39 us (1%)
    pallas_call x1, Pallas kernels, pairs(): pl.pallas_call(functools.partial(pair_kernel, mesh_shape, tiles), in_spec...  25.3 us
    unnamed x19, local copies, waits for them, and re-layouts  24.2 us
    all_to_all x3, starting transfers between devices, swap(): return lax.all_to_all(x, AXES, split_axis=0, concat_axis=0, tiled=True)  19.3 us
    pallas_call x1, Pallas kernels, owner(): pl.pallas_call(functools.partial(owner_kernel, devices, cap), in_specs=[p...  17.6 us
    all_to_all x1, blocking collectives, swap(): return lax.all_to_all(x, AXES, split_axis=0, concat_axis=0, tiled=True)  12.7 us
    pallas_call x1, Pallas kernels, plan(): pl.pallas_call(functools.partial(plan_kernel, devices, cap), out_shape=(j...  12.3 us
    pallas_call x1, Pallas kernels, bucket(): pl.pallas_call(functools.partial(bucket_kernel, devices, cap, rows), out_...  8.52 us
  transfers between devices with their start and end apart: 3, of which 0 were waited for; matrix products, arithmetic and copies ran while one was open for 15% of the time, Pallas kernels for 37%

profile of v1, /device:TPU:0, one launch (start us, length us, event | category | flops | bytes accessed | tf_op | source)
XLA Modules:
  0.0 125.0 jit_solution(9148932371979966033)
XLA Ops:
  0.6 0.7 slice.10
  1.3 0.7 slice.9
  2.0 0.1 reshape.41
  2.1 0.7 convert_element_type.19
  2.8 0.1 convert_element_type.22
  2.9 0.6 all_to_all.23
  3.6 7.3 %all-to-all-start = ((f32[32,1,384]{2,1,0:T(1,128)}), f32[32,1,384]{2,1,0:T(1,128)S(1)}, u32[]{:S(2)}, u32[]{:S(2)}) async-start(f32[32,1,384]{2,1,0:T(1,128)} %all_to_all.23), calls=%async_computation | async-start | bytes 98304 | tf_op jit(solution)/shard_map/all_to_all | solution.py:591
  10.9 0.0 copy-start
  10.9 0.9 copy-done
  11.8 0.0 copy-start.2
  11.8 0.8 copy-done.2
  12.7 12.3 %plan.1 = (f32[3,4096]{1,0:T(4,128)S(1)}, f32[3,4096]{1,0:T(4,128)S(1)}, f32[32,512]{1,0:T(8,128)S(1)}) custom-call(s32[3,4096]{1,0:T(4,128)S(1)} %copy-done.2, s32[512,128]{1,0:T(8,128)S(1)} %bitcast.19), custom_call_target="tpu_custom_call" | custom-call | tf_op jit(solution)/shard_map/plan/pallas_call | solution.py:149
  25.0 0.7 copy.17
  25.7 0.0 all-to-all-done
  25.7 5.8 %all-to-all-start.2 = ((f32[32,1,512]{2,1,0:T(1,128)}), f32[32,1,512]{2,1,0:T(1,128)S(1)}, u32[]{:S(2)}, u32[]{:S(2)}) async-start(f32[32,1,512]{2,1,0:T(1,128)} %copy.17), calls=%async_computation.2 | async-start | bytes 131072 | tf_op jit(solution)/shard_map/all_to_all | solution.py:591
  31.5 0.0 copy-start.1
  31.6 0.8 copy-done.1
  32.4 0.8 copy-done.3
  33.2 0.8 copy-done.4
  34.1 0.8 copy-done.5
  34.8 0.7 copy-done.6
  35.6 0.7 copy-done.7
  36.2 25.3 %pairs.1 = (f32[6,4096]{1,0:T(8,128)S(1)}, f32[3,256]{1,0:T(4,128)S(1)}) custom-call(s32[1]{0:T(128)} %bitcast.1.col_ref, f32[32,384]{1,0:T(8,128)S(1)} %bitcast.20, f32[2,8,128]{2,1,0:T(8,128)S(1)} %copy-done.7, f32[3,4096]{1,0:T(4,128)S(1)} %copy-done.1, f32[3,4096]{1,0:T(4,128)S(1)} %copy-done.3, f32[3,4096]{1,0:T(4,128)S(1)} %copy-done.4, ...), custom_call_target="tpu_custom_call" | custom-call | tf_op jit(solution)/shard_map/pairs/pallas_call | solution.py:384
  61.5 8.5 %bucket.1 = f32[32,24,128]{2,1,0:T(8,128)} custom-call(f32[6,4096]{1,0:T(8,128)S(1)} %get-tuple-element.9.val_ref, f32[3,256]{1,0:T(4,128)S(1)} %get-tuple-element.10.part_ref, f32[3,4096]{1,0:T(4,128)S(1)} %get-tuple-element.11.hp_ref, f32[3,4096]{1,0:T(4,128)S(1)} %get-tuple-element.12.lp_ref), custom_call_target="tpu_custom_call" | custom-call | tf_op jit(solution)/shard_map/bucket/pallas_call | solution.py:466
  70.0 0.0 all-to-all-done.2
  70.0 6.2 %all-to-all-start.1 = ((f32[32,24,128]{2,1,0:T(8,128)}), f32[32,24,128]{2,1,0:T(8,128)S(1)}, u32[]{:S(2)}, u32[]{:S(2)}) async-start(f32[32,24,128]{2,1,0:T(8,128)} %bucket.1), calls=%async_computation.1 | async-start | bytes 786432 | tf_op jit(solution)/shard_map/all_to_all | solution.py:591
  76.3 17.7 %copy.18.morph_ref = f32[300,6,2048]{2,1,0:T(8,128)} copy(f32[300,6,2048]{2,0,1:T(8,128)} %param.20) | data formatting | bytes 29491200 | tf_op args[9]
  94.0 0.0 all-to-all-done.1.inbox_ref
  94.0 17.6 %owner.1 = (f32[6,2048]{1,0:T(8,128)}, f32[32,384]{1,0:T(8,128)S(1)}) custom-call(s32[1]{0:T(128)} %bitcast.me_ref, f32[32,24,128]{2,1,0:T(8,128)S(1)} %all-to-all-done.1.inbox_ref, f32[32,512]{1,0:T(8,128)S(1)} %bitcast.18, f32[300,6,2048]{2,1,0:T(8,128)} %copy.18.morph_ref), custom_call_target="tpu_custom_call" | custom-call | tf_op jit(solution)/shard_map/owner/pallas_call | solution.py:573
  111.6 0.1 copy.19
  111.7 12.7 %all_to_all.36 = f32[32,1,384]{2,1,0:T(1,128)S(1)} all-to-all(f32[32,1,384]{2,1,0:T(1,128)S(1)} %copy.19), channel_id=1, replica_groups=mesh['row'=4,'col'=8] {'row','col'}, dimensions={0} | all-to-all | bytes 98304 | tf_op jit(solution)/shard_map/all_to_all | solution.py:591
  124.4 0.6 reduce_sum.9
  (12 shorter events, 0.1 us)
Async XLA Ops:
  3.6 22.1 %all-to-all-start = ((f32[32,1,384]{2,1,0:T(1,128)}), f32[32,1,384]{2,1,0:T(1,128)S(1)}, u32[]{:S(2)}, u32[]{:S(2)}) async-start(f32[32,1,384]{2,1,0:T(1,128)} %all_to_all.23), calls=%async_computation | async-start | bytes 98304 | tf_op jit(solution)/shard_map/all_to_all | solution.py:591
  10.9 1.0 copy-start
  11.8 0.8 copy-start.2
  25.7 44.3 %all-to-all-start.2 = ((f32[32,1,512]{2,1,0:T(1,128)}), f32[32,1,512]{2,1,0:T(1,128)S(1)}, u32[]{:S(2)}, u32[]{:S(2)}) async-start(f32[32,1,512]{2,1,0:T(1,128)} %copy.17), calls=%async_computation.2 | async-start | bytes 131072 | tf_op jit(solution)/shard_map/all_to_all | solution.py:591
  31.5 0.8 copy-start.1
  32.4 0.8 copy-start.3
  33.2 0.8 copy-start.4
  34.1 0.8 copy-start.5
  34.8 0.7 copy-start.6
  35.5 0.7 copy-start.7
  70.0 24.0 %all-to-all-start.1 = ((f32[32,24,128]{2,1,0:T(8,128)}), f32[32,24,128]{2,1,0:T(8,128)S(1)}, u32[]{:S(2)}, u32[]{:S(2)}) async-start(f32[32,24,128]{2,1,0:T(8,128)} %bucket.1), calls=%async_computation.1 | async-start | bytes 786432 | tf_op jit(solution)/shard_map/all_to_all | solution.py:591
